TPU v7x, 32 devices: a whole 2x2x4 slice. The times are simulated.
32 devices in a mesh: frame: 8 (over z, x), row: 4 (over y, core).
Axes of the slice: x: 2, y: 2, z: 4, core: 2. Of those that a mesh axis runs over, the one named last changes fastest.
Arguments:
- query_in: bfloat16 [32, 4, 8, 2240], P('frame', 'row'), may hold values from -6 to 6
- key_in: bfloat16 [32, 4, 8, 2240], P('frame', 'row'), may hold values from -24 to 24, as said below
- value_in: bfloat16 [32, 4, 8, 2240], P('frame', 'row'), may hold values from -32 to 32, as said below
- hidden_in: bfloat16 [32, 4, 8, 2240], P('frame', 'row'), may hold values from -16 to 16, as said below
- out_weight: bfloat16 [2240, 2240], replicated, may hold values from -0.125 to 0.125
- norm_gain: float32 [2240], replicated, may hold values from 0.25 to 1.75
- temporal_taps: float32 [3, 2240], replicated, may hold values from -3.5 to 3.5
- block_valid: int32 [8], P('frame'), may hold values from 1 to 4, as said below
Outputs:
- mixed: bfloat16 [32, 4, 8, 2240], P('frame', 'row')
Inputs may be any that keep to these rules, and one draw needn't show every extreme that they name: key_in lies within this range. value_in lies within this range. hidden_in lies within this range. `block_valid`: the first frame block is full.
All inputs are finite; a program needn't handle non-finite values.
Results may differ from a plain program's by a relative error of at most 0.0058.
Values may be sent and summed in bfloat16 or wider, within the bound.
A program may use at most 128 MiB of HBM per device.

v0:
```python
import jax
import jax.numpy as jnp
from jax import lax
from jax.sharding import PartitionSpec as P

HEADS = 20
DH = 112


EPS_DEN = 1e-06
EPS_NORM = 1e-06


def entering(part, axis, combine, identity):
    place = lax.axis_index(axis)
    gathered = jax.tree.map(lambda a: lax.all_gather(a, axis), part)
    state = jax.tree.map(lambda a, e: jnp.zeros_like(a) + jnp.asarray(e, a.dtype), part, identity)

    def one(turn, state):
        return combine(
            state, jax.tree.map(lambda a: lax.dynamic_index_in_dim(a, turn, 0, False), gathered)
        )

    return lax.fori_loop(0, place, one, state)


def add_pair(earlier, latter):
    return (earlier[0] + latter[0], earlier[1] + latter[1])


def body(query_in, key_in, value_in, hidden_in, out_weight, norm_gain, temporal_taps, block_valid):
    frames, rows_dev, width_cols, features = query_in.shape
    tokens_dev = frames * rows_dev * width_cols
    frame_mask = (jnp.arange(frames) < block_valid[0]).astype(jnp.float32)
    frame_weight = frame_mask.astype(jnp.bfloat16)[:, None, None, None]
    key_feat = (jnp.maximum(key_in, 0) * frame_weight).reshape(tokens_dev, HEADS, DH)
    value_feat = value_in.reshape(tokens_dev, HEADS, DH)
    local_state = jnp.einsum(
        "thi,thj->hij", key_feat, value_feat, preferred_element_type=jnp.float32
    )
    local_norm = jnp.sum(key_feat, axis=0, dtype=jnp.float32)
    share_state, share_norm = (
        lax.psum_scatter(local_state, "row", scatter_dimension=1, tiled=True),
        lax.psum_scatter(local_norm, "row", scatter_dimension=1, tiled=True),
    )
    identity = (jnp.zeros_like(share_state), jnp.zeros_like(share_norm))
    before_state, before_norm = entering((share_state, share_norm), "frame", add_pair, identity)
    state_share = (before_state + share_state).astype(jnp.bfloat16)
    norm_share = (before_norm + share_norm).astype(jnp.bfloat16)
    total_state, total_norm = (
        lax.all_gather(state_share, "row", axis=1, tiled=True),
        lax.all_gather(norm_share, "row", axis=1, tiled=True),
    )
    query_feat = jnp.maximum(query_in, 0).reshape(tokens_dev, HEADS, DH)
    numerator = jnp.einsum(
        "thi,hij->thj", query_feat, total_state, preferred_element_type=jnp.float32
    )
    denominator = (
        jnp.einsum("thi,hi->th", query_feat, total_norm, preferred_element_type=jnp.float32)
        + EPS_DEN
    )
    token_mask = jnp.broadcast_to(
        frame_mask[:, None, None], (frames, rows_dev, width_cols)
    ).reshape(tokens_dev, 1, 1)
    attended = (
        (numerator / denominator[:, :, None] * token_mask)
        .reshape(tokens_dev, features)
        .astype(jnp.bfloat16)
    )
    projected = jnp.dot(attended, out_weight, preferred_element_type=jnp.float32)
    residual = (hidden_in.reshape(tokens_dev, features).astype(jnp.float32) + projected).astype(
        jnp.bfloat16
    )
    residual_f = lax.optimization_barrier(residual).astype(jnp.float32)
    inverse = lax.rsqrt(jnp.mean(residual_f * residual_f, axis=-1, keepdims=True) + EPS_NORM)
    normed = (
        (residual_f * inverse * norm_gain)
        .astype(jnp.bfloat16)
        .reshape(frames, rows_dev, width_cols, features)
    )
    kernel_taps = temporal_taps.shape[0]
    columns = lax.all_to_all(normed, "frame", split_axis=2, concat_axis=0, tiled=True)
    length_time = columns.shape[0]
    leading = jnp.zeros((kernel_taps - 1,) + columns.shape[1:], jnp.bfloat16)
    extended = jnp.concatenate([leading, columns], axis=0)
    running = jnp.zeros((length_time,) + extended.shape[1:], jnp.float32)
    for offset in range(kernel_taps):
        lower = kernel_taps - 1 - offset
        running = running + temporal_taps[offset] * extended[lower : lower + length_time].astype(
            jnp.float32
        )
    mixed_columns = running.astype(jnp.bfloat16)
    temporal = lax.all_to_all(mixed_columns, "frame", split_axis=0, concat_axis=2, tiled=True)
    temporal_f = lax.optimization_barrier(temporal).astype(jnp.float32)
    mixed = residual_f.reshape(frames, rows_dev, width_cols, features) + temporal_f
    return mixed.astype(jnp.bfloat16)


def solution(mesh):
    placed = (
        P("frame", "row", None, None),
        P("frame", "row", None, None),
        P("frame", "row", None, None),
        P("frame", "row", None, None),
        P(),
        P(),
        P(),
        P("frame"),
    )
    return jax.shard_map(
        body, mesh=mesh, in_specs=placed, out_specs=P("frame", "row", None, None), check_vma=False
    )
```

profile of v0, /device:TPU:0, one launch (start us, length us, event | category | flops | bytes accessed | tf_op | source)
XLA Modules:
  0.0 169.8 jit_solution(6201458012094421040)
XLA Ops:
  6.5 0.0 copy-start.4
  6.5 0.0 copy-start
  6.5 0.0 all-reduce.5.cloned.1.call-start
  7.2 1.0 convert_reduce_fusion
  8.3 0.2 reshape.97
  8.5 1.1 reshape.98
  9.7 1.4 fusion.10
  11.1 0.0 all-reduce.5.cloned.1.call-update
  11.1 0.0 all-gather.6.cloned.1.call-start
  11.1 0.0 copy-done.4
  11.1 0.6 dynamic-slice
  12.4 38.5 %all-reduce.5.cloned.1.call-done = f32[20,112,112]{2,1,0:T(8,128)} async-done(((f32[20,112,112]{2,1,0:T(8,128)}), f32[20,112,112]{2,1,0:T(8,128)}) %all-reduce.5.cloned.1.call-update) | async-done | bytes 1003536
  50.9 1.8 %constant_dynamic-slice_fusion = f32[20,28,112]{2,1,0:T(8,128)} fusion(f32[20,112,112]{2,1,0:T(8,128)} %all-reduce.5.cloned.1.call-done, u32[]{:T(128)S(6)} %multiply.7), kind=kLoop, calls=%fused_computation.42 | loop fusion | bytes 501764
  52.7 0.0 all-gather.6.cloned.1.call-update
  52.7 0.1 reduce_sum.21
  52.8 0.0 copy-done
  52.8 0.2 reshape.99
  53.1 0.1 broadcast_in_dim.8
  53.1 0.1 mul.75
  53.2 10.4 %all-reduce.2 = f32[20,112]{1,0:T(8,128)S(1)} all-reduce(f32[20,112]{1,0:T(8,128)S(1)} %reduce_sum.21), channel_id=5, replica_groups=mesh['frame'=8,'row'=4] {'row'}, use_global_device_ids=true, to_apply=%region_2.0.clone | all-reduce | flops 2240 | bytes 17920
  63.6 0.1 dynamic-slice_bitcast_fusion
  63.7 31.0 %all-gather.2 = f32[8,20,28]{2,1,0:T(8,128)S(1)} all-gather(f32[1,20,28]{2,1,0:T(8,128)S(1)} %dynamic-slice_bitcast_fusion), channel_id=3, replica_groups=mesh['frame'=8,'row'=4] {'frame'}, dimensions={0}, use_global_device_ids=true | all-gather | bytes 20160 | tf_op jit(solution)/shard_map/all_gather | solution.py:16
  94.7 13.7 %all-gather.6.cloned.1.call-done = f32[160,28,112]{2,1,0:T(8,128)} async-done(((f32[20,28,112]{2,1,0:T(8,128)}), f32[160,28,112]{2,1,0:T(8,128)}) %all-gather.6.cloned.1.call-update) | async-done | bytes 2007056 | tf_op jit(solution)/shard_map/all_gather | solution.py:16
  108.5 0.0 copy-start.1
  108.5 0.1 fusion.19
  108.6 5.2 %all-gather.3 = bf16[4,28,20]{1,2,0:T(8,128)(2,1)S(1)} all-gather(bf16[1,28,20]{1,2,0:T(8,128)(2,1)S(1)} %fusion.19), channel_id=1, replica_groups=mesh['frame'=8,'row'=4] {'row'}, dimensions={0}, use_global_device_ids=true | all-gather | bytes 5600 | tf_op jit(solution)/shard_map/all_gather | solution.py:52
  113.8 0.1 reshape.108
  113.9 0.2 fusion.14
  114.0 1.1 add_convert_fusion
  115.1 0.1 copy.34
  115.2 8.2 %all_gather.22 = bf16[20,112,112]{2,0,1:T(8,128)(2,1)S(1)} all-gather(bf16[20,28,112]{2,0,1:T(8,128)(2,1)S(1)} %copy.34), channel_id=1, replica_groups=mesh['frame'=8,'row'=4] {'row'}, dimensions={1}, use_global_device_ids=true | all-gather | bytes 627200 | tf_op jit(solution)/shard_map/all_gather | solution.py:51
  123.3 0.3 fusion.3
  123.6 0.1 copy.38
  123.7 0.2 convert_element_type.83
  123.9 0.0 copy-done.1
  123.9 0.0 copy-start.3
  123.9 0.0 copy-start.2
  123.9 5.6 %fusion = bf16[32,2240]{1,0:T(8,128)(2,1)S(1)} fusion(bf16[32,2240]{1,0:T(8,128)(2,1)S(1)} %convert_element_type.83, bf16[2240,2240]{1,0:T(8,128)(2,1)} %param.14, bf16[4,1,8,2240]{3,2,1,0:T(8,128)(2,1)S(1)} %copy-done.1), kind=kOutput, calls=%fused_computation.3 | convolution fusion | flops 321341440 | bytes 10465280 | tf_op jit(solution)/shard_map/dot_general | solution.py:70
  129.5 0.2 fusion.7
  129.7 0.0 copy-done.3
  129.7 0.1 fusion.13
  129.8 0.7 copy.39
  130.5 11.2 %all-to-all-start = ((bf16[4,1,8,2240]{3,0,1,2:T(4,128)(2,1)}), bf16[4,1,8,2240]{3,0,1,2:T(4,128)(2,1)S(1)}, u32[]{:S(2)}, u32[]{:S(2)}) async-start(bf16[4,1,8,2240]{3,0,1,2:T(4,128)(2,1)} %copy.39), calls=%async_computation | async-start | bytes 294912 | tf_op jit(solution)/shard_map/all_to_all | solution.py:82
  141.7 0.0 copy-done.2
  141.7 0.1 slice_reduce_fusion.2
  141.8 7.7 %all-to-all-done = bf16[4,1,8,2240]{3,0,1,2:T(4,128)(2,1)S(1)} async-done(((bf16[4,1,8,2240]{3,0,1,2:T(4,128)(2,1)}), bf16[4,1,8,2240]{3,0,1,2:T(4,128)(2,1)S(1)}, u32[]{:S(2)}, u32[]{:S(2)}) %all-to-all-start) | async-done | bytes 143392 | tf_op jit(solution)/shard_map/all_to_all | solution.py:82
  149.5 0.1 add_convert_fusion.1
  149.6 0.5 broadcast.61
  150.1 0.7 reduce.8
  150.8 0.2 reshape.122
  151.0 10.0 %all_to_all.36 = bf16[8,2,4480]{2,1,0:T(2,128)(2,1)S(1)} all-to-all(bf16[8,2,4480]{2,1,0:T(2,128)(2,1)S(1)} %reshape.122), channel_id=1, replica_groups=mesh['frame'=8,'row'=4] {'frame'}, dimensions={0} | all-to-all | bytes 286720 | tf_op jit(solution)/shard_map/all_to_all | solution.py:93
  161.0 0.2 reshape.123
  161.3 0.9 reduce.4
  162.2 0.7 fusion.6
  (11 shorter events, 0.2 us)
Async XLA Ops:
  6.5 4.6 %copy-start.4 = (u32[32]{0:T(128)S(1)}, u32[32]{0:T(128)}, u32[]{:S(2)}) copy-start(u32[32]{0:T(128)} %constant.42) | copy-start | bytes 388
  6.5 46.3 %copy-start = (bf16[4,1,8,2240]{3,2,1,0:T(8,128)(2,1)S(1)}, bf16[4,1,8,2240]{3,2,1,0:T(8,128)(2,1)}, u32[]{:S(2)}) copy-start(bf16[4,1,8,2240]{3,2,1,0:T(8,128)(2,1)} %param.10) | copy-start | bytes 430084
  6.5 44.4 %all-reduce.5.cloned.1.call-start = ((), (), s32[]{:S(2)}) async-start(), calls=%async_computation.3 | async-start | bytes 2293760
  11.1 97.3 %all-gather.6.cloned.1.call-start = ((), (), s32[]{:S(2)}) async-start(), calls=%async_computation.2 | async-start | bytes 2949120 | tf_op jit(solution)/shard_map/all_gather | solution.py:16
  108.5 15.4 %copy-start.1 = (bf16[4,1,8,2240]{3,2,1,0:T(8,128)(2,1)S(1)}, bf16[4,1,8,2240]{3,2,1,0:T(8,128)(2,1)}, u32[]{:S(2)}) copy-start(bf16[4,1,8,2240]{3,2,1,0:T(8,128)(2,1)} %param.13) | copy-start | bytes 430084
  123.9 5.8 %copy-start.3 = (f32[2240]{0:T(1024)S(1)}, f32[2240]{0:T(1024)}, u32[]{:S(2)}) copy-start(f32[2240]{0:T(1024)} %param.15) | copy-start | bytes 26884
  123.9 17.8 %copy-start.2 = (f32[3,2240]{1,0:T(4,128)S(1)}, f32[3,2240]{1,0:T(4,128)}, u32[]{:S(2)}) copy-start(f32[3,2240]{1,0:T(4,128)} %param.16) | copy-start | bytes 80644
  130.5 18.9 %all-to-all-start = ((bf16[4,1,8,2240]{3,0,1,2:T(4,128)(2,1)}), bf16[4,1,8,2240]{3,0,1,2:T(4,128)(2,1)S(1)}, u32[]{:S(2)}, u32[]{:S(2)}) async-start(bf16[4,1,8,2240]{3,0,1,2:T(4,128)(2,1)} %copy.39), calls=%async_computation | async-start | bytes 294912 | tf_op jit(solution)/shard_map/all_to_all | solution.py:82
Sparse Core Ops, SparseCore 0:
  11.2 39.6 all-reduce.4
  53.1 55.2 all-gather.5
where the time goes:
time: 170 us
  blocking collectives  64.8 us (38%)
  waiting for transfers between devices  59.9 us (35%)
  between operations  15 us (9%)
  starting transfers between devices  11.2 us (7%)
  matrix products  7.41 us (4%)
  local copies, waits for them, and re-layouts  6.6 us (4%)
  other arithmetic  4.86 us (3%)
    unnamed x3, waiting for transfers between devices  38.6 us
    all_gather x1, blocking collectives, entering(): gathered = jax.tree.map(lambda a: lax.all_gather(a, axis), part)  31 us
    all_gather x1, waiting for transfers between devices, entering(): gathered = jax.tree.map(lambda a: lax.all_gather(a, axis), part)  13.7 us
    all_to_all x1, starting transfers between devices, body(): lax.all_to_all(normed, 'frame', split_axis=2, concat_axis=0, tiled=True)  11.2 us
    unnamed x1, blocking collectives  10.4 us
    all_to_all x1, blocking collectives, body(): lax.all_to_all(mixed_columns, 'frame', split_axis=0, concat_axis=2, tiled...  10 us
    all_gather x1, blocking collectives, body(): lax.all_gather(state_share, 'row', axis=1, tiled=True)  8.15 us
    all_to_all x1, waiting for transfers between devices, body(): lax.all_to_all(normed, 'frame', split_axis=2, concat_axis=0, tiled=True)  7.65 us
  transfers between devices with their start and end apart: 3, of which 3 were waited for; matrix products, arithmetic and copies ran while one was open for 1% of the time, Pallas kernels for 0%

commit v1 on v0

v1 whole, which is shorter than its diff:
```python
import functools

import jax
import jax.numpy as jnp
from jax import lax
from jax.experimental import pallas as pl
from jax.experimental.pallas import tpu as pltpu
from jax.sharding import PartitionSpec as P

HEADS = 20
EPS_DEN = 1e-06
EPS_NORM = 1e-06
LANES = 128
TILE = 256


def kernel(
    n_frame, n_row, group, slots,
    q_hbm, k_hbm, v_hbm, h_hbm, w_hbm, gain_ref, taps_ref, valid_ref,
    out_ref,
    q_in, k_in, v_in, h_in, w_in, kv_out, kv_all, q_out, q_all, state_in, state_out,
    att_out, att_all, att, res, ext,
    in_sem, w_sem, kv_send, kv_recv, q_send, q_recv, s_send, s_recv, a_send, a_recv, halo_sem,
):
    frames, rows_dev, cols, feats = q_in.shape
    tokens = frames * rows_dev * cols
    per_frame = rows_dev * cols
    dh = feats // HEADS
    peers = group * n_row
    planes = n_frame // group
    taps_n = taps_ref.shape[0]
    halo = (taps_n - 1) * per_frame
    bf16, f32 = jnp.bfloat16, jnp.float32

    f, r = lax.axis_index("frame"), lax.axis_index("row")
    plane, inner = f // group, f % group
    me = inner * n_row + r

    def place(rank):
        return {"frame": plane * group + rank // n_row, "row": rank % n_row}

    def at_frame(index):
        return {"frame": index, "row": r}

    def others(step):
        return (me + step) % peers

    loads = [
        pltpu.make_async_copy(src, dst, in_sem.at[i])
        for i, (src, dst) in enumerate(((k_hbm, k_in), (v_hbm, v_in), (q_hbm, q_in), (h_hbm, h_in)))
    ]
    for load in loads:
        load.start()
    barrier = pltpu.get_barrier_semaphore()

    def greet(device):
        pl.semaphore_signal(barrier, inc=1, device_id=device, device_id_type=pl.DeviceIdType.MESH)

    for step in range(1, peers):
        greet(place(others(step)))
    partners = ((f >= group, f - group), (f < n_frame - group, f + group))
    if group > 1:
        partners += (((inner == 0) & (f > 0), f - 1), ((inner == group - 1) & (f < n_frame - 1), f + 1))
    for there, index in partners:
        pl.when(there)(functools.partial(greet, at_frame(index)))

    w_loads = [
        pltpu.make_async_copy(
            w_hbm.at[pl.ds(h * dh, dh), :], w_in.at[h, pl.ds(0, dh), :], w_sem.at[h]
        )
        for h in range(HEADS)
    ]
    for load in w_loads:
        load.start()

    token_frame = lax.broadcasted_iota(jnp.int32, (tokens, 1), 0) // per_frame
    mask = token_frame < valid_ref[0]

    def put(dst, first, value, tail):
        for h in range(peers * slots):
            if h < HEADS:
                full = jnp.concatenate([value[:, h * dh : (h + 1) * dh], tail], axis=1)
            else:
                full = jnp.zeros((tokens, LANES), bf16)
            lane = (h % slots) * LANES
            dst[h // slots, first : first + tokens, lane : lane + LANES] = full

    zeros = jnp.zeros((tokens, LANES - dh), bf16)
    ones = (lax.broadcasted_iota(jnp.int32, (tokens, LANES - dh), 1) == 0).astype(f32).astype(bf16)

    loads[0].wait()
    key = k_in[...].astype(f32).reshape(tokens, feats)
    put(kv_out, 0, jnp.where(mask, jnp.maximum(key, 0.0), 0.0).astype(bf16), zeros)
    loads[1].wait()
    put(kv_out, tokens, v_in[...].astype(f32).reshape(tokens, feats).astype(bf16), ones)

    pl.semaphore_wait(barrier, peers - 1 + sum(there.astype(jnp.int32) for there, _ in partners))

    def exchange(out, all_, send, recv):
        copies = [
            pltpu.make_async_remote_copy(
                src_ref=out.at[others(step)],
                dst_ref=all_.at[me],
                send_sem=send.at[step],
                recv_sem=recv.at[step],
                device_id=place(others(step)),
                device_id_type=pl.DeviceIdType.MESH,
            )
            for step in range(1, peers)
        ]
        for copy in copies:
            copy.start()
        all_[pl.ds(me, 1)] = out[pl.ds(me, 1)]
        return copies

    kv_copies = exchange(kv_out, kv_all, kv_send, kv_recv)

    loads[2].wait()
    query = q_in[...].astype(f32).reshape(tokens, feats)
    put(q_out, 0, jnp.where(mask, jnp.maximum(query, 0.0), 0.0).astype(bf16), zeros)
    q_copies = exchange(q_out, q_all, q_send, q_recv)

    w_in[:, dh:, :] = jnp.zeros((HEADS, LANES - dh, feats), bf16)

    for copy in kv_copies:
        copy.wait_recv()

    block_states = []
    for s in range(slots):
        lane = slice(s * LANES, (s + 1) * LANES)
        mine = []
        for g in range(group):
            ranks = slice(g * n_row, (g + 1) * n_row)
            keys = kv_all[ranks, 0:tokens, lane].reshape(n_row * tokens, LANES)
            values = kv_all[ranks, tokens : 2 * tokens, lane].reshape(n_row * tokens, LANES)
            mine.append(
                lax.dot_general(
                    keys, values, (((0,), (0,)), ((), ())), preferred_element_type=f32
                )[:dh]
            )
        block_states.append(mine)

    def pass_on(s):
        return pltpu.make_async_remote_copy(
            src_ref=state_out.at[s],
            dst_ref=state_in.at[s],
            send_sem=s_send.at[s],
            recv_sem=s_recv.at[s],
            device_id=at_frame(f + group),
            device_id_type=pl.DeviceIdType.MESH,
        )

    @pl.when(plane == 0)
    def _():
        state_in[...] = jnp.zeros(state_in.shape, bf16)

    totals = []
    for s in range(slots):
        pl.when(plane > 0)(lambda s=s: pass_on(s).wait_recv())
        running = state_in[s].astype(f32)
        mine = []
        for g in range(group):
            running = running + block_states[s][g]
            mine.append(running.astype(bf16))
        totals.append(mine)
        state_out[s] = mine[-1]
        pl.when(plane < planes - 1)(lambda s=s: pass_on(s).start())

    for copy in q_copies:
        copy.wait_recv()
    for s in range(slots):
        lane = slice(s * LANES, (s + 1) * LANES)
        for g in range(group):
            ranks = slice(g * n_row, (g + 1) * n_row)
            queries = q_all[ranks, :, lane].reshape(n_row * tokens, LANES)[:, :dh]
            both = jnp.dot(queries, totals[s][g], preferred_element_type=f32)
            value = both / (both[:, dh : dh + 1] + EPS_DEN)
            att_out[ranks, :, lane] = value.astype(bf16).reshape(n_row, tokens, LANES)
    a_copies = exchange(att_out, att_all, a_send, a_recv)

    loads[3].wait()
    for load in w_loads:
        load.wait()
    for copy in a_copies:
        copy.wait_recv()
    depth = HEADS * LANES
    for p in range(peers):
        low = p * slots * LANES
        width = min(slots * LANES, depth - low)
        if width > 0:
            att[:, low : low + width] = att_all[p, :, 0:width]

    def project(start, width):
        weights = w_in[:, :, pl.ds(start, width)].reshape(depth, width)
        projected = jnp.dot(att[...], weights, preferred_element_type=f32)
        hidden = h_in[:, :, :, pl.ds(start, width)].astype(f32).reshape(tokens, width)
        residual = (hidden + projected).astype(bf16).astype(f32)
        res[:, pl.ds(start, width)] = residual
        return jnp.sum(residual * residual, axis=1, keepdims=True)

    whole = feats // TILE

    def tile(i, total):
        return total + project(pl.multiple_of(i * TILE, TILE), TILE)

    square = lax.fori_loop(0, whole, tile, jnp.zeros((tokens, 1), f32))
    if feats % TILE:
        square = square + project(whole * TILE, feats % TILE)
    inverse = lax.rsqrt(square / feats + EPS_NORM)
    gain = gain_ref[...].reshape(1, feats)
    ext[halo:, :] = (res[...] * inverse * gain).astype(bf16)

    to_next = pltpu.make_async_remote_copy(
        src_ref=ext.at[pl.ds(tokens, halo), :],
        dst_ref=ext.at[pl.ds(0, halo), :],
        send_sem=halo_sem.at[0],
        recv_sem=halo_sem.at[1],
        device_id=at_frame(f + 1),
        device_id_type=pl.DeviceIdType.MESH,
    )
    pl.when(f < n_frame - 1)(lambda: to_next.start())

    @pl.when(f == 0)
    def _():
        ext[0:halo, :] = jnp.zeros((halo, feats), bf16)

    pl.when(f > 0)(lambda: to_next.wait_recv())
    normed = ext[...].astype(f32)
    taps = taps_ref[...]
    temporal = jnp.zeros((tokens, feats), f32)
    for j in range(taps_n):
        low = (taps_n - 1 - j) * per_frame
        temporal = temporal + taps[j : j + 1] * normed[low : low + tokens]
    mixed = res[...] + temporal.astype(bf16).astype(f32)
    out_ref[...] = mixed.reshape(out_ref.shape).astype(bf16)

    for copy in kv_copies + q_copies + a_copies:
        copy.wait_send()

    @pl.when(plane < planes - 1)
    def _():
        for s in range(slots):
            pass_on(s).wait_send()

    pl.when(f < n_frame - 1)(lambda: to_next.wait_send())


def body(n_frame, n_row, query_in, key_in, value_in, hidden_in, out_weight, norm_gain, temporal_taps, block_valid):
    frames, rows_dev, cols, feats = query_in.shape
    tokens = frames * rows_dev * cols
    group = 2 if n_frame % 2 == 0 else 1
    peers = group * n_row
    slots = -(-HEADS // peers)
    dh = feats // HEADS
    halo = (temporal_taps.shape[0] - 1) * rows_dev * cols
    width = slots * LANES
    bf16 = jnp.bfloat16
    any_ = pl.BlockSpec(memory_space=pl.ANY)
    vmem = pl.BlockSpec(memory_space=pltpu.VMEM)
    smem = pl.BlockSpec(memory_space=pltpu.SMEM)
    sems = pltpu.SemaphoreType.DMA
    return pl.pallas_call(
        functools.partial(kernel, n_frame, n_row, group, slots),
        out_shape=jax.ShapeDtypeStruct(query_in.shape, bf16),
        in_specs=[any_] * 5 + [vmem, vmem, smem],
        out_specs=vmem,
        scratch_shapes=[
            pltpu.VMEM(query_in.shape, bf16),
            pltpu.VMEM(query_in.shape, bf16),
            pltpu.VMEM(query_in.shape, bf16),
            pltpu.VMEM(query_in.shape, bf16),
            pltpu.VMEM((HEADS, LANES, feats), bf16),
            pltpu.VMEM((peers, 2 * tokens, width), bf16),
            pltpu.VMEM((peers, 2 * tokens, width), bf16),
            pltpu.VMEM((peers, tokens, width), bf16),
            pltpu.VMEM((peers, tokens, width), bf16),
            pltpu.VMEM((slots, dh, LANES), bf16),
            pltpu.VMEM((slots, dh, LANES), bf16),
            pltpu.VMEM((peers, tokens, width), bf16),
            pltpu.VMEM((peers, tokens, width), bf16),
            pltpu.VMEM((tokens, HEADS * LANES), bf16),
            pltpu.VMEM((tokens, feats), jnp.float32),
            pltpu.VMEM((tokens + halo, feats), bf16),
            sems((4,)),
            sems((HEADS,)),
            sems((peers,)),
            sems((peers,)),
            sems((peers,)),
            sems((peers,)),
            sems((slots,)),
            sems((slots,)),
            sems((peers,)),
            sems((peers,)),
            sems((2,)),
        ],
        compiler_params=pltpu.CompilerParams(
            collective_id=0, has_side_effects=True, vmem_limit_bytes=52 * 1024 * 1024
        ),
        cost_estimate=pl.CostEstimate(
            flops=2 * tokens * feats * feats, bytes_accessed=2 * feats * feats, transcendentals=0
        ),
        name="block_forward",
    )(query_in, key_in, value_in, hidden_in, out_weight, norm_gain, temporal_taps, block_valid)


def solution(mesh):
    split = P("frame", "row", None, None)
    placed = (split, split, split, split, P(), P(), P(), P("frame"))
    n_frame, n_row = mesh.shape["frame"], mesh.shape["row"]
    return jax.shard_map(
        functools.partial(body, n_frame, n_row),
        mesh=mesh,
        in_specs=placed,
        out_specs=split,
        check_vma=False,
    )
```

time: 170 us -> 36 us (0.21)
  the two profiles are of different devices: /device:TPU:0 before, /device:TPU:26 now
where the time goes in v1:
time: 36 us; the launch traced here: 35.7 us
  Pallas kernels  29.3 us (81%)
  local copies, waits for them, and re-layouts  5.77 us (16%)
  between operations  0.67 us (2%)
    pallas_call x1, Pallas kernels, body(): pl.pallas_call(functools.partial(kernel, n_frame, n_row, group, slots), o...  29.3 us
    unnamed x13, local copies, waits for them, and re-layouts  5.77 us

profile of v1, /device:TPU:26, one launch (start us, length us, event | category | flops | bytes accessed | tf_op | source)
XLA Modules:
  0.0 35.7 jit_solution(10156987775312280188)
XLA Ops:
  0.7 0.0 copy-start
  0.7 0.9 %copy-done = bf16[4,1,8,2240]{3,2,1,0:T(8,128)(2,1)S(1)} copy-done((bf16[4,1,8,2240]{3,2,1,0:T(8,128)(2,1)S(1)}, bf16[4,1,8,2240]{3,2,1,0:T(8,128)(2,1)}, u32[]{:S(2)}) %copy-start) | copy-done | bytes 143384
  1.6 0.0 copy-start.1
  1.6 0.9 %copy-done.1 = bf16[4,1,8,2240]{3,2,1,0:T(8,128)(2,1)S(1)} copy-done((bf16[4,1,8,2240]{3,2,1,0:T(8,128)(2,1)S(1)}, bf16[4,1,8,2240]{3,2,1,0:T(8,128)(2,1)}, u32[]{:S(2)}) %copy-start.1) | copy-done | bytes 143384
  2.5 0.0 copy-start.2
  2.5 0.9 %copy-done.2 = bf16[4,1,8,2240]{3,2,1,0:T(8,128)(2,1)S(1)} copy-done((bf16[4,1,8,2240]{3,2,1,0:T(8,128)(2,1)S(1)}, bf16[4,1,8,2240]{3,2,1,0:T(8,128)(2,1)}, u32[]{:S(2)}) %copy-start.2) | copy-done | bytes 143384
  3.4 0.0 copy-start.3
  3.4 0.9 %copy-done.3 = bf16[4,1,8,2240]{3,2,1,0:T(8,128)(2,1)S(1)} copy-done((bf16[4,1,8,2240]{3,2,1,0:T(8,128)(2,1)S(1)}, bf16[4,1,8,2240]{3,2,1,0:T(8,128)(2,1)}, u32[]{:S(2)}) %copy-start.3) | copy-done | bytes 143384
  4.3 0.0 copy-start.4
  4.3 0.8 %copy-done.4 = f32[3,2240]{1,0:T(4,128)S(1)} copy-done((f32[3,2240]{1,0:T(4,128)S(1)}, f32[3,2240]{1,0:T(4,128)}, u32[]{:S(2)}) %copy-start.4) | copy-done | bytes 26904
  5.1 0.0 copy-start.5
  5.1 0.7 %copy-done.5 = f32[2240]{0:T(1024)S(1)} copy-done((f32[2240]{0:T(1024)S(1)}, f32[2240]{0:T(1024)}, u32[]{:S(2)}) %copy-start.5) | copy-done | bytes 8984
  5.8 29.3 %block_forward.1 = bf16[4,1,8,2240]{3,2,1,0:T(8,128)(2,1)S(1)} custom-call(bf16[4,1,8,2240]{3,2,1,0:T(8,128)(2,1)S(1)} %copy-done, bf16[4,1,8,2240]{3,2,1,0:T(8,128)(2,1)S(1)} %copy-done.1, bf16[4,1,8,2240]{3,2,1,0:T(8,128)(2,1)S(1)} %copy-done.2, bf16[4,1,8,2240]{3,2,1,0:T(8,128)(2,1)S(1)} %copy-done.3, bf16[2240,2240]{1,0:T(8,128)(2,1)} %w_hbm.1, ...), custom_call_target="tpu_custom_call" | custom-call | flops 321126400 | bytes 10035200 | tf_op jit(solution)/shard_map/block_forward/pallas_call | solution.py:262
  35.1 0.7 %copy.11 = bf16[4,1,8,2240]{3,2,1,0:T(8,128)(2,1)} copy(bf16[4,1,8,2240]{3,2,1,0:T(8,128)(2,1)S(1)} %block_forward.1) | data formatting | bytes 286720
Async XLA Ops:
  0.7 0.9 %copy-start = (bf16[4,1,8,2240]{3,2,1,0:T(8,128)(2,1)S(1)}, bf16[4,1,8,2240]{3,2,1,0:T(8,128)(2,1)}, u32[]{:S(2)}) copy-start(bf16[4,1,8,2240]{3,2,1,0:T(8,128)(2,1)} %q_hbm.1) | copy-start | bytes 430084
  1.6 0.9 %copy-start.1 = (bf16[4,1,8,2240]{3,2,1,0:T(8,128)(2,1)S(1)}, bf16[4,1,8,2240]{3,2,1,0:T(8,128)(2,1)}, u32[]{:S(2)}) copy-start(bf16[4,1,8,2240]{3,2,1,0:T(8,128)(2,1)} %k_hbm.1) | copy-start | bytes 430084
  2.5 0.9 %copy-start.2 = (bf16[4,1,8,2240]{3,2,1,0:T(8,128)(2,1)S(1)}, bf16[4,1,8,2240]{3,2,1,0:T(8,128)(2,1)}, u32[]{:S(2)}) copy-start(bf16[4,1,8,2240]{3,2,1,0:T(8,128)(2,1)} %v_hbm.1) | copy-start | bytes 430084
  3.4 0.9 %copy-start.3 = (bf16[4,1,8,2240]{3,2,1,0:T(8,128)(2,1)S(1)}, bf16[4,1,8,2240]{3,2,1,0:T(8,128)(2,1)}, u32[]{:S(2)}) copy-start(bf16[4,1,8,2240]{3,2,1,0:T(8,128)(2,1)} %h_hbm.1) | copy-start | bytes 430084
  4.3 0.8 %copy-start.4 = (f32[3,2240]{1,0:T(4,128)S(1)}, f32[3,2240]{1,0:T(4,128)}, u32[]{:S(2)}) copy-start(f32[3,2240]{1,0:T(4,128)} %taps_ref.1) | copy-start | bytes 80644
  5.1 0.7 %copy-start.5 = (f32[2240]{0:T(1024)S(1)}, f32[2240]{0:T(1024)}, u32[]{:S(2)}) copy-start(f32[2240]{0:T(1024)} %gain_ref.1) | copy-start | bytes 26884

commit v2 on v1

v2 whole, which is shorter than its diff:
```python
import functools

import jax
import jax.numpy as jnp
from jax import lax
from jax.experimental import pallas as pl
from jax.experimental.pallas import tpu as pltpu
from jax.sharding import PartitionSpec as P

HEADS = 20
EPS_DEN = 1e-06
EPS_NORM = 1e-06
LANES = 128


def kernel(
    n_frame, n_row, group, slots,
    q_hbm, k_hbm, v_hbm, h_hbm, w_hbm, gain_hbm, taps_hbm, valid_ref,
    out_ref,
    q_in, k_in, v_in, h_in, gain_in, taps_in, w_in, kv_out, kv_all, q_out, q_all,
    state, total, state_in, state_out, att_out, att_all, res, ext,
    in_sem, w_sem, kv_send, kv_recv, q_send, q_recv, s_send, s_recv, a_send, a_recv, halo_sem,
):
    frames, rows_dev, cols, feats = q_in.shape
    tokens = frames * rows_dev * cols
    per_frame = rows_dev * cols
    dh = feats // HEADS
    peers = group * n_row
    planes = n_frame // group
    taps_n = taps_in.shape[0]
    halo = (taps_n - 1) * per_frame
    bf16, f32 = jnp.bfloat16, jnp.float32

    f, r = lax.axis_index("frame"), lax.axis_index("row")
    plane, inner = f // group, f % group
    me = inner * n_row + r

    def place(rank):
        return {"frame": plane * group + rank // n_row, "row": rank % n_row}

    def at_frame(index):
        return {"frame": index, "row": r}

    def others(step):
        return (me + step) % peers

    def first(rank):
        return (rank * HEADS + peers - 1) // peers

    def owned(rank):
        return first(rank + 1) - first(rank)

    def where_owned(rank, s, act):
        if s < HEADS // peers:
            act()
        else:
            pl.when(owned(rank) > s)(act)

    def owners(s):
        return [p for p in range(peers) if owned(p) > s]

    loads = [
        pltpu.make_async_copy(src, dst, in_sem.at[i])
        for i, (src, dst) in enumerate(
            (
                (k_hbm, k_in), (v_hbm, v_in), (q_hbm, q_in), (h_hbm, h_in),
                (gain_hbm, gain_in), (taps_hbm, taps_in),
            )
        )
    ]
    for load in loads:
        load.start()
    barrier = pltpu.get_barrier_semaphore()

    def greet(device):
        pl.semaphore_signal(barrier, inc=1, device_id=device, device_id_type=pl.DeviceIdType.MESH)

    for step in range(1, peers):
        greet(place(others(step)))
    partners = ((f >= group, f - group), (f < n_frame - group, f + group))
    if group > 1:
        partners += (((inner == 0) & (f > 0), f - 1), ((inner == group - 1) & (f < n_frame - 1), f + 1))
    for there, index in partners:
        pl.when(there)(functools.partial(greet, at_frame(index)))

    w_loads = []
    w_first = [0]
    for s in range(slots):
        for p in owners(s):
            i = len(w_loads)
            w_loads.append(
                pltpu.make_async_copy(
                    w_hbm.at[pl.ds((first(p) + s) * dh, dh), :], w_in.at[i, pl.ds(0, dh), :], w_sem.at[i]
                )
            )
        w_first.append(len(w_loads))

    token_frame = lax.broadcasted_iota(jnp.int32, (tokens, 1), 0) // per_frame
    mask = token_frame < valid_ref[0]
    zeros = jnp.zeros((tokens, LANES - dh), bf16)
    ones = (lax.broadcasted_iota(jnp.int32, (tokens, LANES - dh), 1) == 0).astype(f32).astype(bf16)

    def put(dst, s, low, value, tail):
        for p in owners(s):
            h = first(p) + s
            dst[s, p, low : low + tokens] = jnp.concatenate([value[:, h * dh : (h + 1) * dh], tail], axis=1)

    def feature(ref):
        return jnp.where(mask, jnp.maximum(ref[...].astype(f32).reshape(tokens, feats), 0.0), 0.0).astype(bf16)

    class Exchange:
        def __init__(self, out, all_, send, recv):
            self.refs = out, all_, send, recv

        def copy(self, s, step):
            out, all_, send, recv = self.refs
            return pltpu.make_async_remote_copy(
                src_ref=out.at[s, others(step)],
                dst_ref=all_.at[s, me],
                send_sem=send.at[s, step],
                recv_sem=recv.at[s, step],
                device_id=place(others(step)),
                device_id_type=pl.DeviceIdType.MESH,
            )

        def start(self, s):
            out, all_, _, _ = self.refs
            for step in range(1, peers):
                where_owned(others(step), s, lambda step=step: self.copy(s, step).start())

            def keep():
                all_[s, pl.ds(me, 1)] = out[s, pl.ds(me, 1)]

            where_owned(me, s, keep)

        def arrived(self, s):
            for step in range(1, peers):
                self.copy(s, step).wait_recv()

        def sent(self, s):
            for step in range(1, peers):
                where_owned(others(step), s, lambda step=step: self.copy(s, step).wait_send())

    kv = Exchange(kv_out, kv_all, kv_send, kv_recv)
    query = Exchange(q_out, q_all, q_send, q_recv)

    loads[0].wait()
    key_feat = feature(k_in)
    loads[1].wait()
    value_feat = v_in[...].astype(f32).reshape(tokens, feats).astype(bf16)
    for s in range(slots):
        put(kv_out, s, 0, key_feat, zeros)
        put(kv_out, s, tokens, value_feat, ones)
        if s == 0:
            pl.semaphore_wait(barrier, peers - 1 + sum(there.astype(jnp.int32) for there, _ in partners))
        kv.start(s)
    for load in w_loads:
        load.start()
    loads[2].wait()
    query_feat = feature(q_in)
    for s in range(slots):
        put(q_out, s, 0, query_feat, zeros)
        query.start(s)
    w_in[:, dh:, :] = jnp.zeros((HEADS, LANES - dh, feats), bf16)

    def pass_on(s):
        return pltpu.make_async_remote_copy(
            src_ref=state_out.at[s],
            dst_ref=state_in.at[s],
            send_sem=s_send.at[s],
            recv_sem=s_recv.at[s],
            device_id=at_frame(f + group),
            device_id_type=pl.DeviceIdType.MESH,
        )

    def ranks(g):
        return slice(g * n_row, (g + 1) * n_row)

    def plane_state(s):
        kv.arrived(s)
        mine = []
        for g in range(group):
            keys = kv_all[s, ranks(g), 0:tokens].reshape(n_row * tokens, LANES)
            values = kv_all[s, ranks(g), tokens : 2 * tokens].reshape(n_row * tokens, LANES)
            mine.append(
                lax.dot_general(
                    keys, values, (((0,), (0,)), ((), ())), preferred_element_type=f32
                )[:dh]
            )
            state[s, g] = mine[-1]

        @pl.when(plane == 0)
        def _():
            state_in[s] = jnp.zeros((dh, LANES), bf16)
            state_out[s] = sum(mine[1:], mine[0]).astype(bf16)
            if planes > 1:
                pass_on(s).start()

    def chain(s):
        pl.when(plane > 0)(lambda: pass_on(s).wait_recv())
        running = state_in[s].astype(f32)
        for g in range(group):
            running = running + state[s, g]
            total[s, g] = running.astype(bf16)

        @pl.when((plane > 0) & (plane < planes - 1))
        def _():
            state_out[s] = running.astype(bf16)
            pass_on(s).start()

    back = Exchange(att_out, att_all, a_send, a_recv)

    def attend(s):
        query.arrived(s)
        for g in range(group):
            queries = q_all[s, ranks(g)].reshape(n_row * tokens, LANES)[:, :dh]
            both = jnp.dot(queries, total[s, g], preferred_element_type=f32)
            value = both / (both[:, dh : dh + 1] + EPS_DEN)
            att_out[s, ranks(g)] = value.astype(bf16).reshape(n_row, tokens, LANES)

    def give_back(s):
        def mine():
            attend(s)
            for step in range(1, peers):
                back_copy(s, step).start()
            att_all[s, pl.ds(me, 1)] = att_out[s, pl.ds(me, 1)]

        where_owned(me, s, mine)

    def back_copy(s, step):
        return back.copy(s, step)

    stages = [(s + lag, lag, s) for s in range(slots) for lag in range(3)]
    for _, lag, s in sorted(stages):
        if lag == 0:
            where_owned(me, s, lambda s=s: plane_state(s))
        elif lag == 1:
            where_owned(me, s, lambda s=s: chain(s))
        else:
            give_back(s)

    loads[3].wait()
    half = -(-feats // (2 * LANES)) * LANES
    square = jnp.zeros((tokens, 1), f32)
    for s in range(slots):
        here = owners(s)
        for load in w_loads[w_first[s] : w_first[s + 1]]:
            load.wait()
        for step in range(1, peers):
            where_owned((me + peers - step) % peers, s, lambda step=step: back_copy(s, step).wait_recv())
        att = jnp.concatenate([att_all[s, p] for p in here], axis=1)
        depth = len(here) * LANES
        for low, high in ((0, half), (half, feats)):
            weights = w_in[w_first[s] : w_first[s + 1], :, low:high].reshape(depth, high - low)
            summed = jnp.dot(att, weights, preferred_element_type=f32)
            if s > 0:
                summed = res[:, low:high] + summed
            if s == slots - 1:
                hidden = h_in[:, :, :, low:high].astype(f32).reshape(tokens, high - low)
                summed = (hidden + summed).astype(bf16).astype(f32)
                square = square + jnp.sum(summed * summed, axis=1, keepdims=True)
            res[:, low:high] = summed
    inverse = lax.rsqrt(square / feats + EPS_NORM)
    loads[4].wait()
    gain = gain_in[...].reshape(1, feats)
    ext[halo:, :] = (res[...] * inverse * gain).astype(bf16)

    to_next = pltpu.make_async_remote_copy(
        src_ref=ext.at[pl.ds(tokens, halo), :],
        dst_ref=ext.at[pl.ds(0, halo), :],
        send_sem=halo_sem.at[0],
        recv_sem=halo_sem.at[1],
        device_id=at_frame(f + 1),
        device_id_type=pl.DeviceIdType.MESH,
    )
    pl.when(f < n_frame - 1)(lambda: to_next.start())

    @pl.when(f == 0)
    def _():
        ext[0:halo, :] = jnp.zeros((halo, feats), bf16)

    for s in range(slots):
        kv.sent(s)
        query.sent(s)

        def gone(s=s):
            for step in range(1, peers):
                back_copy(s, step).wait_send()
            pl.when(plane < planes - 1)(lambda: pass_on(s).wait_send())

        where_owned(me, s, gone)
    loads[5].wait()
    pl.when(f > 0)(lambda: to_next.wait_recv())
    normed = ext[...].astype(f32)
    taps = taps_in[...]
    temporal = jnp.zeros((tokens, feats), f32)
    for j in range(taps_n):
        low = (taps_n - 1 - j) * per_frame
        temporal = temporal + taps[j : j + 1] * normed[low : low + tokens]
    mixed = res[...] + temporal.astype(bf16).astype(f32)
    out_ref[...] = mixed.reshape(out_ref.shape).astype(bf16)
    pl.when(f < n_frame - 1)(lambda: to_next.wait_send())


def body(n_frame, n_row, query_in, key_in, value_in, hidden_in, out_weight, norm_gain, temporal_taps, block_valid):
    frames, rows_dev, cols, feats = query_in.shape
    tokens = frames * rows_dev * cols
    group = 2 if n_frame % 2 == 0 else 1
    peers = group * n_row
    slots = -(-HEADS // peers)
    dh = feats // HEADS
    halo = (temporal_taps.shape[0] - 1) * rows_dev * cols
    bf16, f32 = jnp.bfloat16, jnp.float32
    hbm = pl.BlockSpec(memory_space=pltpu.HBM)
    vmem = pl.BlockSpec(memory_space=pltpu.VMEM)
    smem = pl.BlockSpec(memory_space=pltpu.SMEM)
    sems = pltpu.SemaphoreType.DMA
    return pl.pallas_call(
        functools.partial(kernel, n_frame, n_row, group, slots),
        out_shape=jax.ShapeDtypeStruct(query_in.shape, bf16),
        in_specs=[hbm] * 7 + [smem],
        out_specs=vmem,
        scratch_shapes=[
            pltpu.VMEM(query_in.shape, bf16),
            pltpu.VMEM(query_in.shape, bf16),
            pltpu.VMEM(query_in.shape, bf16),
            pltpu.VMEM(query_in.shape, bf16),
            pltpu.VMEM(norm_gain.shape, f32),
            pltpu.VMEM(temporal_taps.shape, f32),
            pltpu.VMEM((HEADS, LANES, feats), bf16),
            pltpu.VMEM((slots, peers, 2 * tokens, LANES), bf16),
            pltpu.VMEM((slots, peers, 2 * tokens, LANES), bf16),
            pltpu.VMEM((slots, peers, tokens, LANES), bf16),
            pltpu.VMEM((slots, peers, tokens, LANES), bf16),
            pltpu.VMEM((slots, group, dh, LANES), f32),
            pltpu.VMEM((slots, group, dh, LANES), bf16),
            pltpu.VMEM((slots, dh, LANES), bf16),
            pltpu.VMEM((slots, dh, LANES), bf16),
            pltpu.VMEM((slots, peers, tokens, LANES), bf16),
            pltpu.VMEM((slots, peers, tokens, LANES), bf16),
            pltpu.VMEM((tokens, feats), f32),
            pltpu.VMEM((tokens + halo, feats), bf16),
            sems((6,)),
            sems((HEADS,)),
            sems((slots, peers)),
            sems((slots, peers)),
            sems((slots, peers)),
            sems((slots, peers)),
            sems((slots,)),
            sems((slots,)),
            sems((slots, peers)),
            sems((slots, peers)),
            sems((2,)),
        ],
        compiler_params=pltpu.CompilerParams(
            collective_id=0, has_side_effects=True, vmem_limit_bytes=63 * 1024 * 1024
        ),
        cost_estimate=pl.CostEstimate(
            flops=2 * tokens * feats * feats, bytes_accessed=2 * feats * feats, transcendentals=0
        ),
        name="block_forward",
    )(query_in, key_in, value_in, hidden_in, out_weight, norm_gain, temporal_taps, block_valid)


def solution(mesh):
    split = P("frame", "row", None, None)
    placed = (split, split, split, split, P(), P(), P(), P("frame"))
    n_frame, n_row = mesh.shape["frame"], mesh.shape["row"]
    return jax.shard_map(
        functools.partial(body, n_frame, n_row),
        mesh=mesh,
        in_specs=placed,
        out_specs=split,
        check_vma=False,
    )
```

time: 36 us -> 28.8 us (0.80)
  local copies, waits for them, and re-layouts: 5.77 us -> 1.58 us
  Pallas kernels: 29.3 us -> 26.4 us
    unnamed x13 -> x1, local copies, waits for them, and re-layouts: 5.77 us -> 1.58 us
    pallas_call x1, Pallas kernels: 29.3 us -> 26.4 us  [body(): pl.pallas_call(functools.partial(kernel, n_frame, n_row, group, slots), o...]
where the time goes in v2:
time: 28.8 us; the launch traced here: 28.7 us
  Pallas kernels  26.4 us (92%)
  local copies, waits for them, and re-layouts  1.58 us (5%)
  between operations  0.66 us (2%)
    pallas_call x1, Pallas kernels, body(): pl.pallas_call(functools.partial(kernel, n_frame, n_row, group, slots), o...  26.4 us
    unnamed x1, local copies, waits for them, and re-layouts  1.58 us

profile of v2, /device:TPU:26, one launch (start us, length us, event | category | flops | bytes accessed | tf_op | source)
XLA Modules:
  0.0 28.7 jit_solution(6678391460808125970)
XLA Ops:
  0.7 26.4 %block_forward.1 = bf16[4,1,8,2240]{3,2,1,0:T(8,128)(2,1)} custom-call(bf16[4,1,8,2240]{3,2,1,0:T(8,128)(2,1)} %q_hbm.1, bf16[4,1,8,2240]{3,2,1,0:T(8,128)(2,1)} %k_hbm.1, bf16[4,1,8,2240]{3,2,1,0:T(8,128)(2,1)} %v_hbm.1, bf16[4,1,8,2240]{3,2,1,0:T(8,128)(2,1)} %h_hbm.1, bf16[2240,2240]{1,0:T(8,128)(2,1)} %w_hbm.1, f32[2240]{0:T(1024)} %gain_hbm.1, ...), custom_call_target="tpu_custom_call" | custom-call | flops 321126400 | bytes 10035200 | tf_op jit(solution)/shard_map/block_forward/pallas_call | solution.py:318
  27.1 1.6 %copy.11 = bf16[4,1,8,2240]{3,2,1,0:T(8,128)(2,1)} copy(bf16[4,1,8,2240]{3,2,1,0:T(8,128)(2,1)} %block_forward.1) | data formatting | bytes 286720

commit v3 on v2

--- a/solution.py
+++ b/solution.py
@@ -77,9 +77,11 @@
 
     for step in range(1, peers):
         greet(place(others(step)))
-    partners = ((f >= group, f - group), (f < n_frame - group, f + group))
+    for step in range(1, planes):
+        greet(at_frame((f + step * group) % n_frame))
+    partners = ()
     if group > 1:
-        partners += (((inner == 0) & (f > 0), f - 1), ((inner == group - 1) & (f < n_frame - 1), f + 1))
+        partners = (((inner == 0) & (f > 0), f - 1), ((inner == group - 1) & (f < n_frame - 1), f + 1))
     for there, index in partners:
         pl.when(there)(functools.partial(greet, at_frame(index)))
 
@@ -152,26 +154,48 @@
         put(kv_out, s, 0, key_feat, zeros)
         put(kv_out, s, tokens, value_feat, ones)
         if s == 0:
-            pl.semaphore_wait(barrier, peers - 1 + sum(there.astype(jnp.int32) for there, _ in partners))
-        kv.start(s)
+            near = sum(there.astype(jnp.int32) for there, _ in partners)
+            pl.semaphore_wait(barrier, peers - 1 + planes - 1 + near)
+        if s < 2:
+            kv.start(s)
     for load in w_loads:
         load.start()
     loads[2].wait()
     query_feat = feature(q_in)
     for s in range(slots):
         put(q_out, s, 0, query_feat, zeros)
-        query.start(s)
     w_in[:, dh:, :] = jnp.zeros((HEADS, LANES - dh, feats), bf16)
-
-    def pass_on(s):
+    queue = [functools.partial(kv.start, s) for s in range(2, slots)]
+    queue += [functools.partial(query.start, s) for s in range(slots)]
+
+    rounds = range((planes - 1).bit_length())
+
+    def pass_on(s, l, k):
         return pltpu.make_async_remote_copy(
             src_ref=state_out.at[s],
-            dst_ref=state_in.at[s],
-            send_sem=s_send.at[s],
-            recv_sem=s_recv.at[s],
-            device_id=at_frame(f + group),
+            dst_ref=state_in.at[s, l],
+            send_sem=s_send.at[s, k],
+            recv_sem=s_recv.at[s, l],
+            device_id=at_frame(f + (1 + k) * group),
             device_id_type=pl.DeviceIdType.MESH,
         )
+
+    def sender(l):
+        return (plane + 1) % 2 ** (l + 1) == 2**l
+
+    def receiver(l):
+        return (plane // 2**l) % 2 == 1
+
+    def each_target(s, l, act):
+        for k in range(2**l):
+            pl.when(sender(l) & (plane + 1 + k < planes))(lambda k=k: act(pass_on(s, l, k)))
+
+    def send_state(s, l, value):
+        @pl.when(sender(l))
+        def _():
+            state_out[s] = value.astype(bf16)
+
+        each_target(s, l, lambda copy: copy.start())
 
     def ranks(g):
         return slice(g * n_row, (g + 1) * n_row)
@@ -189,24 +213,27 @@
             )
             state[s, g] = mine[-1]
 
-        @pl.when(plane == 0)
-        def _():
-            state_in[s] = jnp.zeros((dh, LANES), bf16)
-            state_out[s] = sum(mine[1:], mine[0]).astype(bf16)
-            if planes > 1:
-                pass_on(s).start()
+        send_state(s, 0, sum(mine[1:], mine[0]))
 
     def chain(s):
-        pl.when(plane > 0)(lambda: pass_on(s).wait_recv())
-        running = state_in[s].astype(f32)
+        running = jnp.zeros((dh, LANES), f32)
+        here = [state[s, g] for g in range(group)]
+        for l in rounds:
+            if l > 0:
+                send_state(s, l, sum(here, running))
+
+            @pl.when(receiver(l))
+            def _():
+                pass_on(s, l, 0).wait_recv()
+
+            @pl.when(jnp.logical_not(receiver(l)))
+            def _():
+                state_in[s, l] = jnp.zeros((dh, LANES), bf16)
+
+            running = running + state_in[s, l].astype(f32)
         for g in range(group):
-            running = running + state[s, g]
+            running = running + here[g]
             total[s, g] = running.astype(bf16)
-
-        @pl.when((plane > 0) & (plane < planes - 1))
-        def _():
-            state_out[s] = running.astype(bf16)
-            pass_on(s).start()
 
     back = Exchange(att_out, att_all, a_send, a_recv)
 
@@ -234,6 +261,8 @@
     for _, lag, s in sorted(stages):
         if lag == 0:
             where_owned(me, s, lambda s=s: plane_state(s))
+            for start in queue[s : s + 1] if s < slots - 1 else queue[s:]:
+                start()
         elif lag == 1:
             where_owned(me, s, lambda s=s: chain(s))
         else:
@@ -286,7 +315,8 @@
         def gone(s=s):
             for step in range(1, peers):
                 back_copy(s, step).wait_send()
-            pl.when(plane < planes - 1)(lambda: pass_on(s).wait_send())
+            for l in rounds:
+                each_target(s, l, lambda copy: copy.wait_send())
 
         where_owned(me, s, gone)
     loads[5].wait()
@@ -308,6 +338,8 @@
     group = 2 if n_frame % 2 == 0 else 1
     peers = group * n_row
     slots = -(-HEADS // peers)
+    planes = n_frame // group
+    rounds = max((planes - 1).bit_length(), 1)
     dh = feats // HEADS
     halo = (temporal_taps.shape[0] - 1) * rows_dev * cols
     bf16, f32 = jnp.bfloat16, jnp.float32
@@ -334,7 +366,7 @@
             pltpu.VMEM((slots, peers, tokens, LANES), bf16),
             pltpu.VMEM((slots, group, dh, LANES), f32),
             pltpu.VMEM((slots, group, dh, LANES), bf16),
-            pltpu.VMEM((slots, dh, LANES), bf16),
+            pltpu.VMEM((slots, rounds, dh, LANES), bf16),
             pltpu.VMEM((slots, dh, LANES), bf16),
             pltpu.VMEM((slots, peers, tokens, LANES), bf16),
             pltpu.VMEM((slots, peers, tokens, LANES), bf16),
@@ -346,8 +378,8 @@
             sems((slots, peers)),
             sems((slots, peers)),
             sems((slots, peers)),
-            sems((slots,)),
-            sems((slots,)),
+            sems((slots, max(planes // 2, 1))),
+            sems((slots, rounds)),
             sems((slots, peers)),
             sems((slots, peers)),
             sems((2,)),

time: 28.8 us -> 29.9 us (1.038)
  the two profiles are of different devices: /device:TPU:26 before, /device:TPU:24 now
where the time goes in v3:
time: 29.9 us; the launch traced here: 29.7 us
  Pallas kernels  27.5 us (92%)
  local copies, waits for them, and re-layouts  1.58 us (5%)
  between operations  0.66 us (2%)
    pallas_call x1, Pallas kernels, body(): pl.pallas_call(functools.partial(kernel, n_frame, n_row, group, slots), o...  27.5 us
    unnamed x1, local copies, waits for them, and re-layouts  1.58 us

profile of v3, /device:TPU:24, one launch (start us, length us, event | category | flops | bytes accessed | tf_op | source)
XLA Modules:
  0.0 29.7 jit_solution(1931606122315367055)
XLA Ops:
  0.7 27.5 %block_forward.1 = bf16[4,1,8,2240]{3,2,1,0:T(8,128)(2,1)} custom-call(bf16[4,1,8,2240]{3,2,1,0:T(8,128)(2,1)} %q_hbm.1, bf16[4,1,8,2240]{3,2,1,0:T(8,128)(2,1)} %k_hbm.1, bf16[4,1,8,2240]{3,2,1,0:T(8,128)(2,1)} %v_hbm.1, bf16[4,1,8,2240]{3,2,1,0:T(8,128)(2,1)} %h_hbm.1, bf16[2240,2240]{1,0:T(8,128)(2,1)} %w_hbm.1, f32[2240]{0:T(1024)} %gain_hbm.1, ...), custom_call_target="tpu_custom_call" | custom-call | flops 321126400 | bytes 10035200 | tf_op jit(solution)/shard_map/block_forward/pallas_call | solution.py:350
  28.1 1.6 %copy.11 = bf16[4,1,8,2240]{3,2,1,0:T(8,128)(2,1)} copy(bf16[4,1,8,2240]{3,2,1,0:T(8,128)(2,1)} %block_forward.1) | data formatting | bytes 286720

commit v4 on v3

--- a/solution.py
+++ b/solution.py
@@ -156,18 +156,15 @@
         if s == 0:
             near = sum(there.astype(jnp.int32) for there, _ in partners)
             pl.semaphore_wait(barrier, peers - 1 + planes - 1 + near)
-        if s < 2:
-            kv.start(s)
+        kv.start(s)
     for load in w_loads:
         load.start()
     loads[2].wait()
     query_feat = feature(q_in)
     for s in range(slots):
         put(q_out, s, 0, query_feat, zeros)
+        query.start(s)
     w_in[:, dh:, :] = jnp.zeros((HEADS, LANES - dh, feats), bf16)
-    queue = [functools.partial(kv.start, s) for s in range(2, slots)]
-    queue += [functools.partial(query.start, s) for s in range(slots)]
-
     rounds = range((planes - 1).bit_length())
 
     def pass_on(s, l, k):
@@ -261,8 +258,6 @@
     for _, lag, s in sorted(stages):
         if lag == 0:
             where_owned(me, s, lambda s=s: plane_state(s))
-            for start in queue[s : s + 1] if s < slots - 1 else queue[s:]:
-                start()
         elif lag == 1:
             where_owned(me, s, lambda s=s: chain(s))
         else:

time: 29.9 us -> 28.8 us (0.963)
  Pallas kernels: 27.5 us -> 26.4 us
    pallas_call x1, Pallas kernels: 27.5 us -> 26.4 us  [body(): pl.pallas_call(functools.partial(kernel, n_frame, n_row, group, slots), o...]
where the time goes in v4:
time: 28.8 us; the launch traced here: 28.6 us
  Pallas kernels  26.4 us (92%)
  local copies, waits for them, and re-layouts  1.58 us (5%)
  between operations  0.66 us (2%)
    pallas_call x1, Pallas kernels, body(): pl.pallas_call(functools.partial(kernel, n_frame, n_row, group, slots), o...  26.4 us
    unnamed x1, local copies, waits for them, and re-layouts  1.58 us

profile of v4, /device:TPU:24, one launch (start us, length us, event | category | flops | bytes accessed | tf_op | source)
XLA Modules:
  0.0 28.6 jit_solution(14770912424328812888)
XLA Ops:
  0.7 26.4 %block_forward.1 = bf16[4,1,8,2240]{3,2,1,0:T(8,128)(2,1)} custom-call(bf16[4,1,8,2240]{3,2,1,0:T(8,128)(2,1)} %q_hbm.1, bf16[4,1,8,2240]{3,2,1,0:T(8,128)(2,1)} %k_hbm.1, bf16[4,1,8,2240]{3,2,1,0:T(8,128)(2,1)} %v_hbm.1, bf16[4,1,8,2240]{3,2,1,0:T(8,128)(2,1)} %h_hbm.1, bf16[2240,2240]{1,0:T(8,128)(2,1)} %w_hbm.1, f32[2240]{0:T(1024)} %gain_hbm.1, ...), custom_call_target="tpu_custom_call" | custom-call | flops 321126400 | bytes 10035200 | tf_op jit(solution)/shard_map/block_forward/pallas_call | solution.py:345
  27.0 1.6 %copy.11 = bf16[4,1,8,2240]{3,2,1,0:T(8,128)(2,1)} copy(bf16[4,1,8,2240]{3,2,1,0:T(8,128)(2,1)} %block_forward.1) | data formatting | bytes 286720

commit v5 on v4

--- a/solution.py
+++ b/solution.py
@@ -68,7 +68,7 @@
             )
         )
     ]
-    for load in loads:
+    for load in loads[:3]:
         load.start()
     barrier = pltpu.get_barrier_semaphore()
 
@@ -77,11 +77,20 @@
 
     for step in range(1, peers):
         greet(place(others(step)))
-    for step in range(1, planes):
-        greet(at_frame((f + step * group) % n_frame))
+    rounds = range((planes - 1).bit_length())
+
+    def sender(l):
+        return (plane + 1) % 2 ** (l + 1) == 2**l
+
+    def receiver(l):
+        return (plane // 2**l) % 2 == 1
+
     partners = ()
+    for l in rounds:
+        partners += tuple((sender(l) & (plane + 1 + k < planes), f + (1 + k) * group) for k in range(2**l))
+        partners += ((receiver(l), (plane // 2**l * 2**l - 1) * group + inner),)
     if group > 1:
-        partners = (((inner == 0) & (f > 0), f - 1), ((inner == group - 1) & (f < n_frame - 1), f + 1))
+        partners += (((inner == 0) & (f > 0), f - 1), ((inner == group - 1) & (f < n_frame - 1), f + 1))
     for there, index in partners:
         pl.when(there)(functools.partial(greet, at_frame(index)))
 
@@ -155,18 +164,16 @@
         put(kv_out, s, tokens, value_feat, ones)
         if s == 0:
             near = sum(there.astype(jnp.int32) for there, _ in partners)
-            pl.semaphore_wait(barrier, peers - 1 + planes - 1 + near)
+            pl.semaphore_wait(barrier, peers - 1 + near)
         kv.start(s)
-    for load in w_loads:
-        load.start()
     loads[2].wait()
     query_feat = feature(q_in)
     for s in range(slots):
         put(q_out, s, 0, query_feat, zeros)
         query.start(s)
+    for load in w_loads + loads[3:]:
+        load.start()
     w_in[:, dh:, :] = jnp.zeros((HEADS, LANES - dh, feats), bf16)
-    rounds = range((planes - 1).bit_length())
-
     def pass_on(s, l, k):
         return pltpu.make_async_remote_copy(
             src_ref=state_out.at[s],
@@ -176,12 +183,6 @@
             device_id=at_frame(f + (1 + k) * group),
             device_id_type=pl.DeviceIdType.MESH,
         )
-
-    def sender(l):
-        return (plane + 1) % 2 ** (l + 1) == 2**l
-
-    def receiver(l):
-        return (plane // 2**l) % 2 == 1
 
     def each_target(s, l, act):
         for k in range(2**l):

time: 28.8 us -> 27.1 us (0.941)
  Pallas kernels: 26.4 us -> 24.7 us
    pallas_call x1, Pallas kernels: 26.4 us -> 24.7 us  [body(): pl.pallas_call(functools.partial(kernel, n_frame, n_row, group, slots), o...]
where the time goes in v5:
time: 27.1 us; the launch traced here: 26.9 us
  Pallas kernels  24.7 us (91%)
  local copies, waits for them, and re-layouts  1.58 us (6%)
  between operations  0.66 us (2%)
    pallas_call x1, Pallas kernels, body(): pl.pallas_call(functools.partial(kernel, n_frame, n_row, group, slots), o...  24.7 us
    unnamed x1, local copies, waits for them, and re-layouts  1.58 us

profile of v5, /device:TPU:24, one launch (start us, length us, event | category | flops | bytes accessed | tf_op | source)
XLA Modules:
  0.0 26.9 jit_solution(15982094463789070049)
XLA Ops:
  0.7 24.7 %block_forward.1 = bf16[4,1,8,2240]{3,2,1,0:T(8,128)(2,1)} custom-call(bf16[4,1,8,2240]{3,2,1,0:T(8,128)(2,1)} %q_hbm.1, bf16[4,1,8,2240]{3,2,1,0:T(8,128)(2,1)} %k_hbm.1, bf16[4,1,8,2240]{3,2,1,0:T(8,128)(2,1)} %v_hbm.1, bf16[4,1,8,2240]{3,2,1,0:T(8,128)(2,1)} %h_hbm.1, bf16[2240,2240]{1,0:T(8,128)(2,1)} %w_hbm.1, f32[2240]{0:T(1024)} %gain_hbm.1, ...), custom_call_target="tpu_custom_call" | custom-call | flops 321126400 | bytes 10035200 | tf_op jit(solution)/shard_map/block_forward/pallas_call | solution.py:346
  25.3 1.6 %copy.11 = bf16[4,1,8,2240]{3,2,1,0:T(8,128)(2,1)} copy(bf16[4,1,8,2240]{3,2,1,0:T(8,128)(2,1)} %block_forward.1) | data formatting | bytes 286720

commit v6 on v5

--- a/solution.py
+++ b/solution.py
@@ -170,10 +170,6 @@
     query_feat = feature(q_in)
     for s in range(slots):
         put(q_out, s, 0, query_feat, zeros)
-        query.start(s)
-    for load in w_loads + loads[3:]:
-        load.start()
-    w_in[:, dh:, :] = jnp.zeros((HEADS, LANES - dh, feats), bf16)
     def pass_on(s, l, k):
         return pltpu.make_async_remote_copy(
             src_ref=state_out.at[s],
@@ -185,7 +181,7 @@
         )
 
     def each_target(s, l, act):
-        for k in range(2**l):
+        for k in reversed(range(2**l)):
             pl.when(sender(l) & (plane + 1 + k < planes))(lambda k=k: act(pass_on(s, l, k)))
 
     def send_state(s, l, value):
@@ -255,14 +251,25 @@
     def back_copy(s, step):
         return back.copy(s, step)
 
-    stages = [(s + lag, lag, s) for s in range(slots) for lag in range(3)]
-    for _, lag, s in sorted(stages):
-        if lag == 0:
-            where_owned(me, s, lambda s=s: plane_state(s))
-        elif lag == 1:
-            where_owned(me, s, lambda s=s: chain(s))
+    relays = functools.reduce(jnp.logical_or, [sender(l) for l in rounds[1:]], plane < 0)
+
+    def forward(s, when):
+        pl.when(when)(lambda: where_owned(me, s, lambda: chain(s)))
+
+    for s in range(slots):
+        where_owned(me, s, lambda s=s: plane_state(s))
+        if s == 0:
+            for later in range(slots):
+                query.start(later)
+            for load in w_loads + loads[3:]:
+                load.start()
+            w_in[:, dh:, :] = jnp.zeros((HEADS, LANES - dh, feats), bf16)
         else:
-            give_back(s)
+            forward(s - 1, relays)
+    forward(slots - 1, relays)
+    for s in range(slots):
+        forward(s, jnp.logical_not(relays))
+        give_back(s)
 
     loads[3].wait()
     half = -(-feats // (2 * LANES)) * LANES

time: 27.1 us -> 26.2 us (0.967)
  Pallas kernels: 24.7 us -> 23.8 us
    pallas_call x1, Pallas kernels: 24.7 us -> 23.8 us  [body(): pl.pallas_call(functools.partial(kernel, n_frame, n_row, group, slots), o...]
where the time goes in v6:
time: 26.2 us; the launch traced here: 26 us
  Pallas kernels  23.8 us (91%)
  local copies, waits for them, and re-layouts  1.58 us (6%)
  between operations  0.66 us (3%)
    pallas_call x1, Pallas kernels, body(): pl.pallas_call(functools.partial(kernel, n_frame, n_row, group, slots), o...  23.8 us
    unnamed x1, local copies, waits for them, and re-layouts  1.58 us

profile of v6, /device:TPU:24, one launch (start us, length us, event | category | flops | bytes accessed | tf_op | source)
XLA Modules:
  0.0 26.0 jit_solution(15310571229065464970)
XLA Ops:
  0.7 23.8 %block_forward.1 = bf16[4,1,8,2240]{3,2,1,0:T(8,128)(2,1)} custom-call(bf16[4,1,8,2240]{3,2,1,0:T(8,128)(2,1)} %q_hbm.1, bf16[4,1,8,2240]{3,2,1,0:T(8,128)(2,1)} %k_hbm.1, bf16[4,1,8,2240]{3,2,1,0:T(8,128)(2,1)} %v_hbm.1, bf16[4,1,8,2240]{3,2,1,0:T(8,128)(2,1)} %h_hbm.1, bf16[2240,2240]{1,0:T(8,128)(2,1)} %w_hbm.1, f32[2240]{0:T(1024)} %gain_hbm.1, ...), custom_call_target="tpu_custom_call" | custom-call | flops 321126400 | bytes 10035200 | tf_op jit(solution)/shard_map/block_forward/pallas_call | solution.py:353
  24.4 1.6 %copy.11 = bf16[4,1,8,2240]{3,2,1,0:T(8,128)(2,1)} copy(bf16[4,1,8,2240]{3,2,1,0:T(8,128)(2,1)} %block_forward.1) | data formatting | bytes 286720

commit v7 on v6

--- a/solution.py
+++ b/solution.py
@@ -311,6 +311,21 @@
     def _():
         ext[0:halo, :] = jnp.zeros((halo, feats), bf16)
 
+    loads[5].wait()
+    taps = taps_in[...]
+
+    def mix(low, high):
+        normed = ext[low : high + halo, :].astype(f32)
+        temporal = jnp.zeros((high - low, feats), f32)
+        for j in range(taps_n):
+            start = (taps_n - 1 - j) * per_frame
+            temporal = temporal + taps[j : j + 1] * normed[start : start + high - low]
+        mixed = res[low:high, :] + temporal.astype(bf16).astype(f32)
+        count = (high - low) // per_frame
+        out_ref[low // per_frame : high // per_frame] = mixed.reshape(count, rows_dev, cols, feats)
+
+    if tokens > halo:
+        mix(halo, tokens)
     for s in range(slots):
         kv.sent(s)
         query.sent(s)
@@ -322,16 +337,8 @@
                 each_target(s, l, lambda copy: copy.wait_send())
 
         where_owned(me, s, gone)
-    loads[5].wait()
     pl.when(f > 0)(lambda: to_next.wait_recv())
-    normed = ext[...].astype(f32)
-    taps = taps_in[...]
-    temporal = jnp.zeros((tokens, feats), f32)
-    for j in range(taps_n):
-        low = (taps_n - 1 - j) * per_frame
-        temporal = temporal + taps[j : j + 1] * normed[low : low + tokens]
-    mixed = res[...] + temporal.astype(bf16).astype(f32)
-    out_ref[...] = mixed.reshape(out_ref.shape).astype(bf16)
+    mix(0, min(halo, tokens))
     pl.when(f < n_frame - 1)(lambda: to_next.wait_send())
 
 
@@ -350,9 +357,9 @@
     vmem = pl.BlockSpec(memory_space=pltpu.VMEM)
     smem = pl.BlockSpec(memory_space=pltpu.SMEM)
     sems = pltpu.SemaphoreType.DMA
-    return pl.pallas_call(
+    mixed = pl.pallas_call(
         functools.partial(kernel, n_frame, n_row, group, slots),
-        out_shape=jax.ShapeDtypeStruct(query_in.shape, bf16),
+        out_shape=jax.ShapeDtypeStruct(query_in.shape, f32),
         in_specs=[hbm] * 7 + [smem],
         out_specs=vmem,
         scratch_shapes=[
@@ -395,6 +402,7 @@
         ),
         name="block_forward",
     )(query_in, key_in, value_in, hidden_in, out_weight, norm_gain, temporal_taps, block_valid)
+    return mixed.astype(bf16)
 
 
 def solution(mesh):

time: 26.2 us -> 26.2 us (level)
  other arithmetic: 0 us -> 1.64 us
  local copies, waits for them, and re-layouts: 1.58 us -> 0 us
    convert_element_type x0 -> x1, other arithmetic: none -> 1.64 us  [body(): return mixed.astype(bf16)]
    unnamed x1 -> x0, local copies, waits for them, and re-layouts: 1.58 us -> none
where the time goes in v7:
time: 26.2 us; the launch traced here: 26.1 us
  Pallas kernels  23.8 us (91%)
  other arithmetic  1.64 us (6%)
  between operations  0.66 us (3%)
    pallas_call x1, Pallas kernels, body(): pl.pallas_call(functools.partial(kernel, n_frame, n_row, group, slots), o...  23.8 us
    convert_element_type x1, other arithmetic, body(): return mixed.astype(bf16)  1.64 us

profile of v7, /device:TPU:24, one launch (start us, length us, event | category | flops | bytes accessed | tf_op | source)
XLA Modules:
  0.0 26.1 jit_solution(17012802026083195292)
XLA Ops:
  0.7 23.8 %block_forward.1 = f32[4,1,8,2240]{3,2,1,0:T(8,128)} custom-call(bf16[4,1,8,2240]{3,2,1,0:T(8,128)(2,1)} %q_hbm.1, bf16[4,1,8,2240]{3,2,1,0:T(8,128)(2,1)} %k_hbm.1, bf16[4,1,8,2240]{3,2,1,0:T(8,128)(2,1)} %v_hbm.1, bf16[4,1,8,2240]{3,2,1,0:T(8,128)(2,1)} %h_hbm.1, bf16[2240,2240]{1,0:T(8,128)(2,1)} %w_hbm.1, f32[2240]{0:T(1024)} %gain_hbm.1, ...), custom_call_target="tpu_custom_call" | custom-call | flops 321126400 | bytes 10035200 | tf_op jit(solution)/shard_map/block_forward/pallas_call | solution.py:360
  24.4 1.6 %convert_element_type.3 = bf16[4,1,8,2240]{3,2,1,0:T(8,128)(2,1)} convert(f32[4,1,8,2240]{3,2,1,0:T(8,128)} %block_forward.1) | non-fusion elementwise | flops 71680 | bytes 430080 | tf_op jit(solution)/shard_map/convert_element_type | solution.py:405

commit v8 on v7

--- a/solution.py
+++ b/solution.py
@@ -68,7 +68,7 @@
             )
         )
     ]
-    for load in loads[:3]:
+    for load in loads[:2]:
         load.start()
     barrier = pltpu.get_barrier_semaphore()
 
@@ -94,6 +94,7 @@
     for there, index in partners:
         pl.when(there)(functools.partial(greet, at_frame(index)))
 
+    loads[2].start()
     w_loads = []
     w_first = [0]
     for s in range(slots):
@@ -295,8 +296,7 @@
     inverse = lax.rsqrt(square / feats + EPS_NORM)
     loads[4].wait()
     gain = gain_in[...].reshape(1, feats)
-    ext[halo:, :] = (res[...] * inverse * gain).astype(bf16)
-
+    ext[tokens:, :] = (res[tokens - halo :, :] * inverse[tokens - halo :] * gain).astype(bf16)
     to_next = pltpu.make_async_remote_copy(
         src_ref=ext.at[pl.ds(tokens, halo), :],
         dst_ref=ext.at[pl.ds(0, halo), :],
@@ -306,6 +306,8 @@
         device_id_type=pl.DeviceIdType.MESH,
     )
     pl.when(f < n_frame - 1)(lambda: to_next.start())
+    if tokens > halo:
+        ext[halo:tokens, :] = (res[: tokens - halo, :] * inverse[: tokens - halo] * gain).astype(bf16)
 
     @pl.when(f == 0)
     def _():
@@ -322,7 +324,7 @@
             temporal = temporal + taps[j : j + 1] * normed[start : start + high - low]
         mixed = res[low:high, :] + temporal.astype(bf16).astype(f32)
         count = (high - low) // per_frame
-        out_ref[low // per_frame : high // per_frame] = mixed.reshape(count, rows_dev, cols, feats)
+        out_ref[low // per_frame : high // per_frame] = mixed.reshape(count, rows_dev, cols, feats).astype(bf16)
 
     if tokens > halo:
         mix(halo, tokens)
@@ -357,9 +359,9 @@
     vmem = pl.BlockSpec(memory_space=pltpu.VMEM)
     smem = pl.BlockSpec(memory_space=pltpu.SMEM)
     sems = pltpu.SemaphoreType.DMA
-    mixed = pl.pallas_call(
+    return pl.pallas_call(
         functools.partial(kernel, n_frame, n_row, group, slots),
-        out_shape=jax.ShapeDtypeStruct(query_in.shape, f32),
+        out_shape=jax.ShapeDtypeStruct(query_in.shape, bf16),
         in_specs=[hbm] * 7 + [smem],
         out_specs=vmem,
         scratch_shapes=[
@@ -402,7 +404,6 @@
         ),
         name="block_forward",
     )(query_in, key_in, value_in, hidden_in, out_weight, norm_gain, temporal_taps, block_valid)
-    return mixed.astype(bf16)
 
 
 def solution(mesh):

time: 26.2 us -> 26.1 us (level)
  other arithmetic: 1.64 us -> 0 us
  local copies, waits for them, and re-layouts: 0 us -> 1.58 us
    convert_element_type x1 -> x0, other arithmetic: 1.64 us -> none  [body(): return mixed.astype(bf16)]
    unnamed x0 -> x1, local copies, waits for them, and re-layouts: none -> 1.58 us
where the time goes in v8:
time: 26.1 us; the launch traced here: 26 us
  Pallas kernels  23.7 us (91%)
  local copies, waits for them, and re-layouts  1.58 us (6%)
  between operations  0.66 us (3%)
    pallas_call x1, Pallas kernels, body(): pl.pallas_call(functools.partial(kernel, n_frame, n_row, group, slots), o...  23.7 us
    unnamed x1, local copies, waits for them, and re-layouts  1.58 us

profile of v8, /device:TPU:24, one launch (start us, length us, event | category | flops | bytes accessed | tf_op | source)
XLA Modules:
  0.0 26.0 jit_solution(11293406333398222933)
XLA Ops:
  0.7 23.7 %block_forward.1 = bf16[4,1,8,2240]{3,2,1,0:T(8,128)(2,1)} custom-call(bf16[4,1,8,2240]{3,2,1,0:T(8,128)(2,1)} %q_hbm.1, bf16[4,1,8,2240]{3,2,1,0:T(8,128)(2,1)} %k_hbm.1, bf16[4,1,8,2240]{3,2,1,0:T(8,128)(2,1)} %v_hbm.1, bf16[4,1,8,2240]{3,2,1,0:T(8,128)(2,1)} %h_hbm.1, bf16[2240,2240]{1,0:T(8,128)(2,1)} %w_hbm.1, f32[2240]{0:T(1024)} %gain_hbm.1, ...), custom_call_target="tpu_custom_call" | custom-call | flops 321126400 | bytes 10035200 | tf_op jit(solution)/shard_map/block_forward/pallas_call | solution.py:362
  24.4 1.6 %copy.11 = bf16[4,1,8,2240]{3,2,1,0:T(8,128)(2,1)} copy(bf16[4,1,8,2240]{3,2,1,0:T(8,128)(2,1)} %block_forward.1) | data formatting | bytes 286720

commit v9 on v8

--- a/solution.py
+++ b/solution.py
@@ -259,13 +259,13 @@
 
     for s in range(slots):
         where_owned(me, s, lambda s=s: plane_state(s))
-        if s == 0:
+        if s == min(1, slots - 1):
             for later in range(slots):
                 query.start(later)
             for load in w_loads + loads[3:]:
                 load.start()
             w_in[:, dh:, :] = jnp.zeros((HEADS, LANES - dh, feats), bf16)
-        else:
+        if s > 0:
             forward(s - 1, relays)
     forward(slots - 1, relays)
     for s in range(slots):

time: 26.1 us -> 26.1 us (level)
  no operation moved by 1% of the time
where the time goes in v9:
time: 26.1 us; the launch traced here: 25.9 us
  Pallas kernels  23.7 us (91%)
  local copies, waits for them, and re-layouts  1.58 us (6%)
  between operations  0.66 us (3%)
    pallas_call x1, Pallas kernels, body(): pl.pallas_call(functools.partial(kernel, n_frame, n_row, group, slots), o...  23.7 us
    unnamed x1, local copies, waits for them, and re-layouts  1.58 us

profile of v9, /device:TPU:24, one launch (start us, length us, event | category | flops | bytes accessed | tf_op | source)
XLA Modules:
  0.0 25.9 jit_solution(1890216933970206481)
XLA Ops:
  0.7 23.7 %block_forward.1 = bf16[4,1,8,2240]{3,2,1,0:T(8,128)(2,1)} custom-call(bf16[4,1,8,2240]{3,2,1,0:T(8,128)(2,1)} %q_hbm.1, bf16[4,1,8,2240]{3,2,1,0:T(8,128)(2,1)} %k_hbm.1, bf16[4,1,8,2240]{3,2,1,0:T(8,128)(2,1)} %v_hbm.1, bf16[4,1,8,2240]{3,2,1,0:T(8,128)(2,1)} %h_hbm.1, bf16[2240,2240]{1,0:T(8,128)(2,1)} %w_hbm.1, f32[2240]{0:T(1024)} %gain_hbm.1, ...), custom_call_target="tpu_custom_call" | custom-call | flops 321126400 | bytes 10035200 | tf_op jit(solution)/shard_map/block_forward/pallas_call | solution.py:362
  24.4 1.6 %copy.11 = bf16[4,1,8,2240]{3,2,1,0:T(8,128)(2,1)} copy(bf16[4,1,8,2240]{3,2,1,0:T(8,128)(2,1)} %block_forward.1) | data formatting | bytes 286720
